TPU v7x, 256 devices: a whole 4x4x8 slice. The times are simulated.
256 devices in a mesh: beam: 128 (over x_hi, y, z, core), tm: 2 (over x_lo).
Axes of the slice: x: 4 (x_hi: 2, x_lo: 2; x = x_hi * 2 + x_lo), y: 4, z: 8, core: 2. Of those that a mesh axis runs over, the one named last changes fastest.
Arguments:
- voltages: bfloat16 [2, 16, 8192, 2048], P(None, 'tm', 'beam'), may hold values from -6 to 6
- feed_slot: int32 [2048], replicated, may hold values from 0 to 2047, each once
- tree_shift: int32 [14], replicated, may hold values from 0 to 4, as said below
Outputs:
- search: float32 [1024, 2, 16, 512], P('beam', None, 'tm')
Inputs may be any that keep to these rules, and one draw needn't show every extreme that they name: `feed_slot`: every grid slot holds exactly one feed. `tree_shift`: the entries 2^(s+1) - 2 to 2^(s+2) - 3 are the lags of section s for trials k = 0 .. 2^(s+1) - 1; each lies between 0 and 2^s, and the last trial of every section has lag exactly 2^s.
All inputs are finite; a program needn't handle non-finite values.
Results may differ from a plain program's by a relative error of at most 0.00083.
Values sent between devices are 32-bit elements; how exact they have to be, the bound alone decides.
A program may use at most 128 MiB of HBM per device.

v0:
```python
import math

import jax
import jax.numpy as jnp
import numpy as np
from jax import lax
from jax.experimental import pallas as pl
from jax.experimental.pallas import tpu as pltpu
from jax.sharding import PartitionSpec as P

POL = 2
EW = 4
NS = 256
FEEDS = 2048
FSUM = 16
LEVELS = 3
BOXES = 2
FRAMES = 8
CHANS = 64
SAMPLES = FRAMES * CHANS
BANDS = CHANS // FSUM
LANES = 128
MESH = pl.DeviceIdType.MESH


def steer_table():
    index = np.arange(NS)
    phase = (index[:, None] * index[None, :]) % NS
    angle = phase.astype(np.float32) * np.float32(2.0 * math.pi / NS)
    order = [high * 16 + core * 8 + low for core in range(2) for high in range(16) for low in range(8)]
    cos_table = np.cos(angle).astype(np.float32)[order]
    sin_table = np.sin(angle).astype(np.float32)[order]
    top = np.concatenate([cos_table, sin_table], axis=1)
    bottom = np.concatenate([-sin_table, cos_table], axis=1)
    return jnp.asarray(np.concatenate([top, bottom], axis=0), jnp.bfloat16)


def bin_table():
    table = np.zeros((BANDS * FRAMES, SAMPLES), np.float32)
    for frame in range(FRAMES):
        for chan in range(CHANS):
            table[(chan // FSUM) * FRAMES + frame, frame * CHANS + chan] = 0.5 / FEEDS
    return jnp.asarray(table, jnp.bfloat16)


def beams_kernel(slot_ref, volt_ref, steer_ref, bin_ref, eye_ref, out_ref, turned, gridded, north, power):
    contract_last = (((1,), (1,)), ((), ()))
    for part in range(4):
        rows = volt_ref[pl.ds(part * 256, 256), :]
        for block in range(8):
            flipped = lax.dot_general(
                eye_ref[...], rows[:, block * 256 : block * 256 + 256], contract_last,
                preferred_element_type=jnp.float32,
            )
            for half in range(2):
                turned[pl.ds(block * 2048 + part * 2 + half, 256, stride=8), :] = flipped[
                    :, half * LANES : half * LANES + LANES
                ]

    def move(feed, carry):
        slot = slot_ref[feed]
        gridded[pl.ds(pl.multiple_of(slot * 8, 8), 8), :] = turned[pl.ds(pl.multiple_of(feed * 8, 8), 8), :]
        return carry

    lax.fori_loop(0, FEEDS, move, 0, unroll=16)

    for pol in range(POL):
        for cyl in range(EW):
            first = (pol * EW + cyl) * NS * 8
            parts = [gridded[pl.ds(first + q, NS, stride=8), :].astype(jnp.bfloat16) for q in range(8)]
            both = jnp.concatenate(
                [jnp.concatenate(parts[:4], axis=1), jnp.concatenate(parts[4:], axis=1)], axis=0
            )
            north[cyl] = jnp.dot(steer_ref[...], both, preferred_element_type=jnp.float32)
        for strip in range(16):
            top = pl.ds(strip * 16, 16)
            low = pl.ds(NS + strip * 16, 16)
            re = [north[cyl, top, :] for cyl in range(EW)]
            im = [north[cyl, low, :] for cyl in range(EW)]
            even_re, even_im = re[0] + re[2], im[0] + im[2]
            odd_re, odd_im = re[0] - re[2], im[0] - im[2]
            side_re, side_im = re[1] + re[3], im[1] + im[3]
            diff_re, diff_im = re[1] - re[3], im[1] - im[3]
            sums = [
                (even_re + side_re, even_im + side_im),
                (odd_re + diff_im, odd_im - diff_re),
                (even_re - side_re, even_im - side_im),
                (odd_re - diff_im, odd_im + diff_re),
            ]
            for column in range(EW):
                energy = sums[column][0] * sums[column][0] + sums[column][1] * sums[column][1]
                if pol == 0:
                    power[column, top, :] = energy
                else:
                    power[column, top, :] += energy
    for column in range(EW):
        whole = power[column]
        high = whole.astype(jnp.bfloat16)
        rest = (whole - high.astype(jnp.float32)).astype(jnp.bfloat16)
        binned = lax.dot_general(
            bin_ref[...], high, contract_last, preferred_element_type=jnp.float32
        ) + lax.dot_general(bin_ref[...], rest, contract_last, preferred_element_type=jnp.float32)
        for core in range(2):
            out_ref[core * 2 + column // 2, column % 2] = binned[:, core * LANES : core * LANES + LANES]


def beams(voltages, feed_slot):
    return pl.pallas_call(
        beams_kernel,
        out_shape=jax.ShapeDtypeStruct((4, 2, BANDS * FRAMES, LANES), jnp.float32),
        in_specs=[pl.BlockSpec(memory_space=pltpu.SMEM)] + [pl.BlockSpec(memory_space=pltpu.VMEM)] * 4,
        out_specs=pl.BlockSpec(memory_space=pltpu.VMEM),
        scratch_shapes=[
            pltpu.VMEM((FEEDS * 8, LANES), jnp.float32),
            pltpu.VMEM((FEEDS * 8, LANES), jnp.float32),
            pltpu.VMEM((EW, 2 * NS, SAMPLES), jnp.float32),
            pltpu.VMEM((EW, NS, SAMPLES), jnp.float32),
        ],
        compiler_params=pltpu.CompilerParams(vmem_limit_bytes=48 * 2**20),
        name="beams",
    )(
        feed_slot,
        voltages.reshape(2 * SAMPLES, FEEDS),
        steer_table(),
        bin_table(),
        jnp.asarray(np.eye(256), jnp.bfloat16),
    )


def swap_chunks(tiles):
    lane = lax.broadcasted_iota(jnp.int32, (8, LANES), 1)
    tiles = list(tiles)
    for bit in range(4):
        span = 8 << bit
        low_half = (lane // span) % 2 == 0
        for first in range(16):
            if first >> bit & 1:
                continue
            second = first | 1 << bit
            one, two = tiles[first], tiles[second]
            tiles[first] = jnp.where(low_half, one, pltpu.roll(two, span, 1))
            tiles[second] = jnp.where(low_half, pltpu.roll(one, LANES - span, 1), two)
    return tiles


def search_kernel(
    shift_ref, own_ref, out_ref, level_0, level_1, level_2, series, packed, landed, result,
    near_send, near_recv, far_send, far_recv, self_sem, out_sem,
):
    place = lax.axis_index("beam")
    half = lax.axis_index("tm")
    core = lax.rem(place, 2)
    site = lax.div(place, 2)
    sites = lax.axis_size("beam") // 2
    side = lax.div(site, 32)
    own_slot = side == half

    landed[:, 4:8, :] = jnp.zeros((sites, 4, LANES), jnp.float32)
    barrier = pltpu.get_barrier_semaphore()

    def peer(c, h):
        return (site * 2 + c, h)

    for other in range(1, 4):
        c = lax.rem(core + other // 2, 2)
        h = lax.rem(half + other % 2, 2)
        pl.semaphore_signal(barrier, inc=1, device_id=peer(c, h), device_id_type=MESH)

    def greet(step, carry):
        from_site = lax.rem(site + step, sites)

        @pl.when(jnp.logical_not(jnp.logical_and(from_site == site, own_slot)))
        def _():
            pl.semaphore_signal(barrier, inc=1, device_id=(from_site * 2 + core, side), device_id_type=MESH)

        return carry

    lax.fori_loop(0, sites, greet, 0)
    pl.semaphore_wait(barrier, jnp.where(own_slot, sites + 2, sites + 3))

    here = (
        slice(None),
        pl.ds(core * BANDS, BANDS),
        pl.ds(pl.multiple_of(half * FRAMES, FRAMES), FRAMES),
        slice(None),
    )
    copies = []
    for other in range(1, 4):
        c = lax.rem(core + other // 2, 2)
        h = lax.rem(half + other % 2, 2)
        copy = pltpu.make_async_remote_copy(
            src_ref=own_ref.at[c * 2 + h],
            dst_ref=level_0.at[here],
            send_sem=near_send.at[other],
            recv_sem=near_recv.at[other],
            device_id=peer(c, h),
            device_id_type=MESH,
        )
        copy.start()
        copies.append(copy)
    mine = pltpu.make_async_copy(own_ref.at[core * 2 + half], level_0.at[here], self_sem)
    mine.start()
    for buffer in (level_0, level_1, level_2):
        buffer[:, :, 16:24, :] = jnp.zeros((2, 8, 8, LANES), jnp.float32)
    mine.wait()
    for copy in copies:
        copy.wait()

    buffers = (level_0, level_1, level_2)
    for level in range(LEVELS):
        span = 2**level
        current = buffers[level]
        for band in range(8):
            base, k = band - band % (2 * span), band % (2 * span)
            lower = base + k // 2
            lag = shift_ref[2 * span - 2 + k]
            for column in range(2):
                total = (
                    current[column, lower, 0:16, :] + current[column, lower + span, pl.ds(lag, 16), :]
                )
                if level < LEVELS - 1:
                    buffers[level + 1][column, band, 0:16, :] = total
                else:
                    series[column, pl.ds(band, 16, stride=8), :] = total
    lane = lax.broadcasted_iota(jnp.int32, (8, LANES), 1)
    row = lax.broadcasted_iota(jnp.int32, (8, LANES), 0)
    keep = (lane < LANES // 2) == (row < 4)
    for column in range(2):
        flipped = jnp.transpose(series[column])
        for target in range(16):
            tile = flipped[target * 8 : target * 8 + 8]
            crossed = pltpu.roll(pltpu.roll(tile, 4, 0), LANES // 2, 1)
            packed[column * 16 + target] = jnp.where(keep, tile, crossed)

    def to_early(target):
        return pltpu.make_async_remote_copy(
            src_ref=packed.at[target],
            dst_ref=landed.at[site],
            send_sem=far_send.at[0],
            recv_sem=far_recv,
            device_id=((half * 32 + target) * 2 + core, 0),
            device_id_type=MESH,
        )

    def to_late(target):
        return pltpu.make_async_remote_copy(
            src_ref=packed.at[target, 4:8],
            dst_ref=landed.at[site, 0:4],
            send_sem=far_send.at[1],
            recv_sem=far_recv,
            device_id=((half * 32 + target) * 2 + core, 1),
            device_id_type=MESH,
        )

    def send(step, carry):
        target = lax.rem(site + step, 32)
        is_self = half * 32 + target == site

        @pl.when(jnp.logical_not(jnp.logical_and(is_self, half == 0)))
        def _():
            to_early(target).start()

        @pl.when(jnp.logical_not(jnp.logical_and(is_self, half == 1)))
        def _():
            to_late(target).start()

        return carry

    lax.fori_loop(0, 32, send, 0)
    own_target = lax.rem(site, 32)

    @pl.when(jnp.logical_and(own_slot, half == 0))
    def _():
        copy = pltpu.make_async_copy(packed.at[own_target], landed.at[site], self_sem)
        copy.start()
        copy.wait()

    @pl.when(jnp.logical_and(own_slot, half == 1))
    def _():
        copy = pltpu.make_async_copy(packed.at[own_target, 4:8], landed.at[site, 0:4], self_sem)
        copy.start()
        copy.wait()

    def wait_recv(count, rows):
        pltpu.make_async_copy(landed.at[0:count, 0:rows], landed.at[0:count, 0:rows], far_recv).wait()

    @pl.when(half == 0)
    def _():
        @pl.when(own_slot)
        def _():
            wait_recv(sites - 1, 8)

        @pl.when(jnp.logical_not(own_slot))
        def _():
            wait_recv(sites, 8)

    @pl.when(half == 1)
    def _():
        @pl.when(own_slot)
        def _():
            wait_recv(sites - 1, 4)

        @pl.when(jnp.logical_not(own_slot))
        def _():
            wait_recv(sites, 4)

    writes = []
    for block in range(4):
        tiles = swap_chunks([landed[block * 16 + g] for g in range(16)])
        for high in range(2):
            for frame in range(8):
                now = tiles[high * 8 + frame]
                if frame < 7:
                    later = tiles[high * 8 + frame + 1]
                else:
                    later = pltpu.roll(tiles[high * 8], 4, 0)
                first = high * 64 + frame
                result[block, pl.ds(first, 4, stride=16), :] = (now * (1.0 / (FSUM * 8)))[0:4]
                result[block, pl.ds(first + 8, 4, stride=16), :] = ((now + later) * (1.0 / (FSUM * 16)))[0:4]

        write = pltpu.make_async_copy(result.at[block], out_ref.at[:, pl.ds(block * LANES, LANES)], out_sem.at[block])
        write.start()
        writes.append(write)

    def wait_send(index, count, rows):
        pltpu.make_async_copy(packed.at[0:count, 0:rows], packed.at[0:count, 0:rows], far_send.at[index]).wait()

    early_self = jnp.logical_and(own_slot, half == 0)
    late_self = jnp.logical_and(own_slot, half == 1)
    for flag, index, rows in ((early_self, 0, 8), (late_self, 1, 4)):
        @pl.when(flag)
        def _():
            wait_send(index, 31, rows)

        @pl.when(jnp.logical_not(flag))
        def _():
            wait_send(index, 32, rows)

    for write in writes:
        write.wait()


def search(binned, tree_shift):
    level = pltpu.VMEM((2, 8, 24, LANES), jnp.float32)
    return pl.pallas_call(
        search_kernel,
        out_shape=jax.ShapeDtypeStruct((8 * BOXES * FRAMES, 512), jnp.float32),
        in_specs=[pl.BlockSpec(memory_space=pltpu.SMEM), pl.BlockSpec(memory_space=pltpu.VMEM)],
        out_specs=pl.BlockSpec(memory_space=pl.ANY),
        scratch_shapes=[
            level,
            level,
            level,
            pltpu.VMEM((2, 128, LANES), jnp.float32),
            pltpu.VMEM((32, 8, LANES), jnp.float32),
            pltpu.VMEM((64, 8, LANES), jnp.float32),
            pltpu.VMEM((4, 128, LANES), jnp.float32),
            pltpu.SemaphoreType.DMA((4,)),
            pltpu.SemaphoreType.DMA((4,)),
            pltpu.SemaphoreType.DMA((2,)),
            pltpu.SemaphoreType.DMA,
            pltpu.SemaphoreType.DMA,
            pltpu.SemaphoreType.DMA((4,)),
        ],
        compiler_params=pltpu.CompilerParams(
            collective_id=0, has_side_effects=True, vmem_limit_bytes=16 * 2**20
        ),
        name="search",
    )(tree_shift, binned.reshape(4, 2, BANDS, FRAMES, LANES))


def on_device(voltages, feed_slot, tree_shift):
    binned = beams(voltages, feed_slot)
    result = search(binned, tree_shift)
    return result.reshape(8, BOXES, FRAMES, 512)


def solution(mesh):
    placed = (P(None, "tm", "beam", None), P(), P())
    return jax.shard_map(
        on_device,
        mesh=mesh,
        in_specs=placed,
        out_specs=P("beam", None, "tm", None),
        check_vma=False,
    )
```

profile of v0, /device:TPU:1, one launch (start us, length us, event | category | flops | bytes accessed | tf_op | source)
XLA Modules:
  0.0 41.4 jit_solution(5646359193698311609)
XLA Ops:
  0.0 0.0 copy-start.5
  0.0 0.0 copy-start
  0.0 2.2 %copy-done = bf16[2,8,64,2048]{3,2,1,0:T(8,128)(2,1)S(1)} copy-done((bf16[2,8,64,2048]{3,2,1,0:T(8,128)(2,1)S(1)}, bf16[2,8,64,2048]{3,2,1,0:T(8,128)(2,1)}, u32[]{:S(2)}) %copy-start) | copy-done | bytes 4194328
  2.2 0.0 copy-start.1
  2.2 1.0 %copy-done.1 = bf16[512,512]{1,0:T(8,128)(2,1)S(1)} copy-done((bf16[512,512]{1,0:T(8,128)(2,1)S(1)}, bf16[512,512]{1,0:T(8,128)(2,1)}, u32[]{:S(2)}) %copy-start.1) | copy-done | bytes 524312
  3.2 0.0 copy-start.2
  3.2 0.9 %copy-done.2 = bf16[256,256]{1,0:T(8,128)(2,1)S(1)} copy-done((bf16[256,256]{1,0:T(8,128)(2,1)S(1)}, bf16[256,256]{1,0:T(8,128)(2,1)}, u32[]{:S(2)}) %copy-start.2) | copy-done | bytes 131096
  4.2 0.0 copy-start.3
  4.2 0.8 %copy-done.3 = bf16[32,512]{1,0:T(8,128)(2,1)S(1)} copy-done((bf16[32,512]{1,0:T(8,128)(2,1)S(1)}, bf16[32,512]{1,0:T(8,128)(2,1)}, u32[]{:S(2)}) %copy-start.3) | copy-done | bytes 32792
  4.9 0.0 copy-start.4
  4.9 0.7 %copy-done.4 = s32[2048]{0:T(1024)S(1)} copy-done((s32[2048]{0:T(1024)S(1)}, s32[2048]{0:T(1024)}, u32[]{:S(2)}) %copy-start.4) | copy-done | bytes 8216
  5.6 9.1 %beams.1 = f32[4,2,32,128]{3,2,1,0:T(8,128)S(1)} custom-call(s32[2048]{0:T(1024)S(1)} %copy-done.4, bf16[1024,2048]{1,0:T(8,128)(2,1)S(1)} %bitcast.3, bf16[512,512]{1,0:T(8,128)(2,1)S(1)} %copy-done.1, bf16[32,512]{1,0:T(8,128)(2,1)S(1)} %copy-done.3, bf16[256,256]{1,0:T(8,128)(2,1)S(1)} %copy-done.2), custom_call_target="tpu_custom_call" | custom-call | tf_op jit(solution)/shard_map/beams/pallas_call | solution.py:108
  14.7 0.0 copy-done.5
  14.7 26.0 %search.1 = f32[128,512]{1,0:T(8,128)S(1)} custom-call(s32[14]{0:T(128)S(1)} %copy-done.5, f32[4,2,4,8,128]{4,3,2,1,0:T(8,128)S(1)} %bitcast.5), custom_call_target="tpu_custom_call" | custom-call | tf_op jit(solution)/shard_map/search/pallas_call | solution.py:345
  40.7 0.7 %copy.8 = f32[8,2,8,512]{3,2,1,0:T(8,128)} copy(f32[8,2,8,512]{3,2,1,0:T(8,128)S(1)} %bitcast.4) | data formatting | bytes 524288
Async XLA Ops:
  0.0 14.7 %copy-start.5 = (s32[14]{0:T(128)S(1)}, s32[14]{0:T(128)}, u32[]{:S(2)}) copy-start(s32[14]{0:T(128)} %shift_ref.1) | copy-start | bytes 172
  0.0 2.2 %copy-start = (bf16[2,8,64,2048]{3,2,1,0:T(8,128)(2,1)S(1)}, bf16[2,8,64,2048]{3,2,1,0:T(8,128)(2,1)}, u32[]{:S(2)}) copy-start(bf16[2,8,64,2048]{3,2,1,0:T(8,128)(2,1)} %param.6) | copy-start | bytes 12582916
  2.2 1.0 %copy-start.1 = (bf16[512,512]{1,0:T(8,128)(2,1)S(1)}, bf16[512,512]{1,0:T(8,128)(2,1)}, u32[]{:S(2)}) copy-start(bf16[512,512]{1,0:T(8,128)(2,1)} %constant.6.clone.steer_ref) | copy-start | bytes 1572868
  3.2 0.9 %copy-start.2 = (bf16[256,256]{1,0:T(8,128)(2,1)S(1)}, bf16[256,256]{1,0:T(8,128)(2,1)}, u32[]{:S(2)}) copy-start(bf16[256,256]{1,0:T(8,128)(2,1)} %constant.8.clone.eye_ref) | copy-start | bytes 393220
  4.2 0.8 %copy-start.3 = (bf16[32,512]{1,0:T(8,128)(2,1)S(1)}, bf16[32,512]{1,0:T(8,128)(2,1)}, u32[]{:S(2)}) copy-start(bf16[32,512]{1,0:T(8,128)(2,1)} %constant.7.clone.bin_ref) | copy-start | bytes 98308
  4.9 0.7 %copy-start.4 = (s32[2048]{0:T(1024)S(1)}, s32[2048]{0:T(1024)}, u32[]{:S(2)}) copy-start(s32[2048]{0:T(1024)} %slot_ref.1) | copy-start | bytes 24580
where the time goes:
time: 41.7 us; the launch traced here: 41.4 us
  Pallas kernels  35.1 us (84%)
  local copies, waits for them, and re-layouts  6.32 us (15%)
    pallas_call x1, Pallas kernels, search(): pl.pallas_call(search_kernel, out_shape=jax.ShapeDtypeStruct((8 * BOXES *...  26 us
    pallas_call x1, Pallas kernels, beams(): pl.pallas_call(beams_kernel, out_shape=jax.ShapeDtypeStruct((4, 2, BANDS...  9.06 us
    unnamed x13, local copies, waits for them, and re-layouts  6.32 us

commit v1 on v0

v1 whole, which is shorter than its diff:
```python
import math

import jax
import jax.numpy as jnp
import ml_dtypes
import numpy as np
from jax import lax
from jax.experimental import pallas as pl
from jax.experimental.pallas import tpu as pltpu
from jax.sharding import PartitionSpec as P

POL = 2
EW = 4
NS = 256
FEEDS = 2048
FSUM = 16
LEVELS = 3
BOXES = 2
FRAMES = 8
CHANS = 64
SAMPLES = FRAMES * CHANS
BANDS = CHANS // FSUM
MEMBERS = 16
LANES = 128
MESH = pl.DeviceIdType.MESH


def steer_tables():
    index = np.arange(NS)
    phase = (index[:, None] * index[None, :]) % NS
    angle = phase.astype(np.float32) * np.float32(2.0 * math.pi / NS)
    order = [high * 16 + core * 8 + low for core in range(2) for high in range(16) for low in range(8)]
    both = np.concatenate([np.cos(angle)[order], np.sin(angle)[order]], axis=1)
    return jnp.asarray(both.astype(ml_dtypes.bfloat16).astype(np.float32))


def contract_last(left, right):
    return lax.dot_general(left, right, (((1,), (1,)), ((), ())), preferred_element_type=jnp.float32)


def iota(shape, dim):
    return lax.broadcasted_iota(jnp.int32, shape, dim)


def swap_chunks(tiles):
    lane = lax.broadcasted_iota(jnp.int32, (8, LANES), 1)
    tiles = list(tiles)
    for bit in range(4):
        span = 8 << bit
        low_half = (lane // span) % 2 == 0
        for first in range(16):
            if first >> bit & 1:
                continue
            second = first | 1 << bit
            one, two = tiles[first], tiles[second]
            tiles[first] = jnp.where(low_half, one, pltpu.roll(two, span, 1))
            tiles[second] = jnp.where(low_half, pltpu.roll(one, LANES - span, 1), two)
    return tiles


def search_kernel(
    slot_hbm, shift_hbm, volt_hbm, tables_hbm, out_ref,
    slot, owner_vmem, owner, shift_ref, volts, tables, turned, gridded, north,
    own_ref, near, level_0, level_1, level_2, series, packed, landed, result,
    slot_sem, owner_sem, shift_sem, volt_sem, steer_sem,
    near_send, near_recv, far_send, far_recv, self_sem, out_sem,
):
    slot_copy = pltpu.make_async_copy(slot_hbm, slot, slot_sem)
    steer_copy = pltpu.make_async_copy(tables_hbm, tables, steer_sem)
    shift_copy = pltpu.make_async_copy(shift_hbm, shift_ref, shift_sem)
    volt_copies = [
        pltpu.make_async_copy(volt_hbm.at[pl.ds(part * 256, 256)], volts.at[pl.ds(part * 256, 256)], volt_sem.at[part])
        for part in range(4)
    ]
    for copy in [slot_copy] + volt_copies + [steer_copy, shift_copy]:
        copy.start()

    landed[:, :, 4:8, :] = jnp.zeros((16, 4, 4, LANES), jnp.float32)
    for buffer in (level_0, level_1, level_2):
        buffer[:, :, 16:24, :] = jnp.zeros((2, 8, 8, LANES), jnp.float32)
    place = lax.axis_index("beam")
    half = lax.axis_index("tm")
    core = lax.rem(place, 2)
    site = lax.div(place, 2)
    z = lax.rem(site, 8)
    y = lax.rem(lax.div(site, 8), 4)
    x_high = lax.div(site, 32)
    member = (core * 2 + half) * 4 + y
    selfish = x_high == half

    def of_member(other):
        c, h, at = lax.div(other, 8), lax.rem(lax.div(other, 4), 2), lax.rem(other, 4)
        return (((x_high * 4 + at) * 8 + z) * 2 + c, h)

    def at_site(xx, zz, h):
        return (((xx * 4 + y) * 8 + zz) * 2 + core, h)

    barrier = pltpu.get_barrier_semaphore()

    def greet(step, carry):
        pl.semaphore_signal(
            barrier, inc=1, device_id=of_member(lax.rem(member + step, MEMBERS)), device_id_type=MESH
        )
        return carry

    lax.fori_loop(1, MEMBERS, greet, 0)

    def greet_far(step, carry):
        xx, zz = lax.div(step, 8), lax.rem(z + step, 8)

        @pl.when(jnp.logical_not(jnp.logical_and(jnp.logical_and(xx == x_high, zz == z), selfish)))
        def _():
            pl.semaphore_signal(barrier, inc=1, device_id=at_site(xx, zz, x_high), device_id_type=MESH)

        return carry

    lax.fori_loop(0, 16, greet_far, 0)
    slot_copy.wait()
    places = iota((FEEDS // LANES, LANES), 0) * LANES + iota((FEEDS // LANES, LANES), 1)
    found = [jnp.zeros((FEEDS // LANES, LANES), jnp.int32) for _ in range(4)]
    for part in range(4):
        volt_copies[part].wait()
        rows = volts[pl.ds(part * 256, 256), :]
        for block in range(8):
            flipped = jnp.transpose(rows[:, block * 256 : block * 256 + 256]).astype(jnp.float32)
            for half_rows in range(2):
                turned[pl.ds(block * 2048 + part * 2 + half_rows, 256, stride=8), :] = flipped[
                    :, half_rows * LANES : half_rows * LANES + LANES
                ]
            if part < 2:
                row = part * 8 + block
                for lane in range(LANES):
                    found[lane % 4] = jnp.where(places == slot[row, lane], row * LANES + lane, found[lane % 4])
        if part == 1:
            owner_vmem[...] = jnp.maximum(jnp.maximum(found[0], found[1]), jnp.maximum(found[2], found[3]))
            owner_copy = pltpu.make_async_copy(owner_vmem, owner, owner_sem)
            owner_copy.start()

    owner_copy.wait()

    def move(row, carry):
        for lane in range(LANES):
            feed = owner[row, lane]
            first = pl.multiple_of((row * LANES + lane) * 8, 8)
            gridded[pl.ds(first, 8), :] = turned[pl.ds(feed * 8, 8), :]
        return carry

    lax.fori_loop(0, FEEDS // LANES, move, 0)

    steer_copy.wait()
    top = tables[...].astype(jnp.bfloat16)
    steer = jnp.concatenate([top, jnp.concatenate([-top[:, NS:], top[:, :NS]], axis=1)], axis=0)
    for pol in range(POL):
        for cyl in range(EW):
            first = (pol * EW + cyl) * NS * 8
            parts = [gridded[pl.ds(first + q, NS, stride=8), :].astype(jnp.bfloat16) for q in range(8)]
            both = jnp.concatenate(
                [jnp.concatenate(parts[:4], axis=1), jnp.concatenate(parts[4:], axis=1)], axis=0
            )
            north[pol * EW + cyl] = jnp.dot(steer, both, preferred_element_type=jnp.float32)

    bin_row, sample = iota((BANDS * FRAMES, SAMPLES), 0), iota((BANDS * FRAMES, SAMPLES), 1)
    chosen = (sample // CHANS == bin_row % FRAMES) & (sample % CHANS // FSUM == bin_row // FRAMES)
    adder = jnp.where(chosen, 0.5 / FEEDS, 0.0).astype(jnp.bfloat16)
    binned = [[] for _ in range(EW)]
    for strip in range(2):
        energies = [[] for _ in range(EW)]
        for piece in range(8):
            top = pl.ds(strip * 128 + piece * 16, 16)
            low = pl.ds(NS + strip * 128 + piece * 16, 16)
            power = [None] * EW
            for pol in range(POL):
                re = [north[pol * EW + cyl, top, :] for cyl in range(EW)]
                im = [north[pol * EW + cyl, low, :] for cyl in range(EW)]
                even_re, even_im = re[0] + re[2], im[0] + im[2]
                odd_re, odd_im = re[0] - re[2], im[0] - im[2]
                side_re, side_im = re[1] + re[3], im[1] + im[3]
                diff_re, diff_im = re[1] - re[3], im[1] - im[3]
                sums = [
                    (even_re + side_re, even_im + side_im),
                    (odd_re + diff_im, odd_im - diff_re),
                    (even_re - side_re, even_im - side_im),
                    (odd_re - diff_im, odd_im + diff_re),
                ]
                for column in range(EW):
                    energy = sums[column][0] * sums[column][0] + sums[column][1] * sums[column][1]
                    power[column] = energy if pol == 0 else power[column] + energy
            for column in range(EW):
                energies[column].append(power[column])
        for column in range(EW):
            whole = jnp.concatenate(energies[column], axis=0)
            high = whole.astype(jnp.bfloat16)
            rest = (whole - high.astype(jnp.float32)).astype(jnp.bfloat16)
            binned[column].append(contract_last(adder, high) + contract_last(adder, rest))
    low_lanes = iota((16, LANES), 1) < LANES // 2
    for column in range(EW):
        for c in range(2):
            one, two = binned[column][c][0:16], binned[column][c][16:32]
            target = (c * 2 + column // 2) * 4 + column % 2 * 2
            own_ref[target] = jnp.where(low_lanes, one, pltpu.roll(two, LANES // 2, 1))
            own_ref[target + 1] = jnp.where(low_lanes, pltpu.roll(one, LANES // 2, 1), two)


    pl.semaphore_wait(barrier, jnp.where(selfish, MEMBERS + 14, MEMBERS + 15))

    def near_copy(other):
        return pltpu.make_async_remote_copy(
            src_ref=own_ref.at[other],
            dst_ref=near.at[member],
            send_sem=near_send,
            recv_sem=near_recv,
            device_id=of_member(other),
            device_id_type=MESH,
        )

    def send_near(step, carry):
        near_copy(lax.rem(member + step, MEMBERS)).start()
        return carry

    lax.fori_loop(1, MEMBERS, send_near, 0)
    mine = pltpu.make_async_copy(own_ref.at[member], near.at[member], self_sem)
    mine.start()
    mine.wait()
    pltpu.make_async_copy(near.at[0:15], near.at[0:15], near_recv).wait()

    shift_copy.wait()
    low_frames = iota((FRAMES, LANES), 1) < LANES // 2
    for c in range(2):
        for h in range(2):
            for pair in range(2):
                first = (c * 2 + h) * 4 + pair * 2
                for low in range(2):
                    one, two = near[first, low * 8 : low * 8 + 8, :], near[first + 1, low * 8 : low * 8 + 8, :]
                    frames = slice(h * 8, h * 8 + 8)
                    level_0[pair, c * 4 + low, frames, :] = jnp.where(low_frames, one, pltpu.roll(two, LANES // 2, 1))
                    level_0[pair, c * 4 + 2 + low, frames, :] = jnp.where(
                        low_frames, pltpu.roll(one, LANES // 2, 1), two
                    )

    buffers = (level_0, level_1, level_2)
    for level in range(LEVELS):
        span = 2**level
        current = buffers[level]
        for band in range(8):
            base, k = band - band % (2 * span), band % (2 * span)
            lower = base + k // 2
            lag = shift_ref[2 * span - 2 + k]
            for pair in range(2):
                total = current[pair, lower, 0:16, :] + current[pair, lower + span, pl.ds(lag, 16), :]
                if level < LEVELS - 1:
                    buffers[level + 1][pair, band, 0:16, :] = total
                else:
                    series[pair, pl.ds(band, 16, stride=8), :] = total
    keep = (iota((8, LANES), 1) < LANES // 2) == (iota((8, LANES), 0) < 4)
    for pair in range(2):
        flipped = jnp.transpose(series[pair])
        for low in range(2):
            for target in range(8):
                first = low * 64 + target * 8
                tile = flipped[first : first + 8]
                crossed = pltpu.roll(pltpu.roll(tile, 4, 0), LANES // 2, 1)
                packed[target, pair * 2 + low] = jnp.where(keep, tile, crossed)

    slot = x_high * 8 + z

    def to_early(target):
        return pltpu.make_async_remote_copy(
            src_ref=packed.at[target],
            dst_ref=landed.at[slot],
            send_sem=far_send.at[0],
            recv_sem=far_recv,
            device_id=at_site(half, target, 0),
            device_id_type=MESH,
        )

    def to_late(target):
        return pltpu.make_async_remote_copy(
            src_ref=packed.at[target, :, 4:8],
            dst_ref=landed.at[slot, :, 0:4],
            send_sem=far_send.at[1],
            recv_sem=far_recv,
            device_id=at_site(half, target, 1),
            device_id_type=MESH,
        )

    early_self = jnp.logical_and(selfish, half == 0)
    late_self = jnp.logical_and(selfish, half == 1)

    def send(step, carry):
        target = lax.rem(z + step, 8)

        @pl.when(jnp.logical_not(jnp.logical_and(target == z, early_self)))
        def _():
            to_early(target).start()

        @pl.when(jnp.logical_not(jnp.logical_and(target == z, late_self)))
        def _():
            to_late(target).start()

        return carry

    lax.fori_loop(0, 8, send, 0)

    @pl.when(early_self)
    def _():
        copy = pltpu.make_async_copy(packed.at[z], landed.at[slot], self_sem)
        copy.start()
        copy.wait()

    @pl.when(late_self)
    def _():
        copy = pltpu.make_async_copy(packed.at[z, :, 4:8], landed.at[slot, :, 0:4], self_sem)
        copy.start()
        copy.wait()

    def wait_for(buffer, sem, count, rows):
        part = buffer.at[0:count, :, 0:rows]
        pltpu.make_async_copy(part, part, sem).wait()

    for h, rows in ((0, 8), (1, 4)):
        @pl.when(jnp.logical_and(half == h, selfish))
        def _():
            wait_for(landed, far_recv, 15, rows)

        @pl.when(jnp.logical_and(half == h, jnp.logical_not(selfish)))
        def _():
            wait_for(landed, far_recv, 16, rows)

    writes = []
    for block in range(4):
        xx, pair = block // 2, block % 2
        tiles = swap_chunks([landed[xx * 8 + zz, pair * 2 + low] for low in range(2) for zz in range(8)])
        for high in range(2):
            for frame in range(8):
                now = tiles[high * 8 + frame]
                if frame < 7:
                    later = tiles[high * 8 + frame + 1]
                else:
                    later = pltpu.roll(tiles[high * 8], 4, 0)
                first = high * 64 + frame
                result[block, pl.ds(first, 4, stride=16), :] = (now * (1.0 / (FSUM * 8)))[0:4]
                result[block, pl.ds(first + 8, 4, stride=16), :] = ((now + later) * (1.0 / (FSUM * 16)))[0:4]
        write = pltpu.make_async_copy(result.at[block], out_ref.at[:, pl.ds(block * LANES, LANES)], out_sem.at[block])
        write.start()
        writes.append(write)

    pltpu.make_async_copy(own_ref.at[0:15], own_ref.at[0:15], near_send).wait()
    for flag, index, rows in ((early_self, 0, 8), (late_self, 1, 4)):
        @pl.when(flag)
        def _():
            wait_for(packed, far_send.at[index], 7, rows)

        @pl.when(jnp.logical_not(flag))
        def _():
            wait_for(packed, far_send.at[index], 8, rows)

    for write in writes:
        write.wait()


def search(voltages, feed_slot, tree_shift):
    level = pltpu.VMEM((2, 8, 24, LANES), jnp.float32)
    dma = pltpu.SemaphoreType.DMA
    return pl.pallas_call(
        search_kernel,
        out_shape=jax.ShapeDtypeStruct((8 * BOXES * FRAMES, 512), jnp.float32),
        in_specs=[pl.BlockSpec(memory_space=pltpu.HBM)] * 4,
        out_specs=pl.BlockSpec(memory_space=pl.ANY),
        scratch_shapes=[
            pltpu.SMEM((FEEDS // LANES, LANES), jnp.int32),
            pltpu.VMEM((FEEDS // LANES, LANES), jnp.int32),
            pltpu.SMEM((FEEDS // LANES, LANES), jnp.int32),
            pltpu.SMEM((14,), jnp.int32),
            pltpu.VMEM((2 * SAMPLES, FEEDS), jnp.bfloat16),
            pltpu.VMEM((NS, 2 * NS), jnp.float32),
            pltpu.VMEM((FEEDS * 8, LANES), jnp.float32),
            pltpu.VMEM((FEEDS * 8, LANES), jnp.float32),
            pltpu.VMEM((POL * EW, 2 * NS, SAMPLES), jnp.float32),
            pltpu.VMEM((MEMBERS, 16, LANES), jnp.float32),
            pltpu.VMEM((MEMBERS, 16, LANES), jnp.float32),
            level,
            level,
            level,
            pltpu.VMEM((2, 128, LANES), jnp.float32),
            pltpu.VMEM((8, 4, 8, LANES), jnp.float32),
            pltpu.VMEM((16, 4, 8, LANES), jnp.float32),
            pltpu.VMEM((4, 128, LANES), jnp.float32),
            dma,
            dma,
            dma,
            dma((4,)),
            dma,
            dma,
            dma,
            dma((2,)),
            dma,
            dma,
            dma((4,)),
        ],
        compiler_params=pltpu.CompilerParams(
            collective_id=0, has_side_effects=True, vmem_limit_bytes=60 * 2**20
        ),
        name="search",
    )(
        feed_slot.reshape(FEEDS // LANES, LANES),
        tree_shift,
        voltages.reshape(2 * SAMPLES, FEEDS),
        steer_tables(),
    )


def on_device(voltages, feed_slot, tree_shift):
    result = search(voltages, feed_slot, tree_shift)
    return result.reshape(8, BOXES, FRAMES, 512)


def solution(mesh):
    placed = (P(None, "tm", "beam", None), P(), P())
    return jax.shard_map(
        on_device,
        mesh=mesh,
        in_specs=placed,
        out_specs=P("beam", None, "tm", None),
        check_vma=False,
    )
```

time: 41.7 us -> 34 us (0.82)
  local copies, waits for them, and re-layouts: 6.32 us -> 1.67 us
  Pallas kernels: 35.1 us -> 31.9 us
    pallas_call x1 -> x0, Pallas kernels: 9.06 us -> none  [beams(): pl.pallas_call(beams_kernel, out_shape=jax.ShapeDtypeStruct((4, 2, BANDS...]
    pallas_call x1, Pallas kernels: 26 us -> 31.9 us  [search(): pl.pallas_call(search_kernel, out_shape=jax.ShapeDtypeStruct((8 * BOXES *...]
    unnamed x13 -> x1, local copies, waits for them, and re-layouts: 6.32 us -> 1.67 us
where the time goes in v1:
time: 34 us; the launch traced here: 33.6 us
  Pallas kernels  31.9 us (94%)
  local copies, waits for them, and re-layouts  1.67 us (5%)
    pallas_call x1, Pallas kernels, search(): pl.pallas_call(search_kernel, out_shape=jax.ShapeDtypeStruct((8 * BOXES *...  31.9 us
    unnamed x1, local copies, waits for them, and re-layouts  1.67 us

profile of v1, /device:TPU:1, one launch (start us, length us, event | category | flops | bytes accessed | tf_op | source)
XLA Modules:
  0.0 33.6 jit_solution(13674991548696057076)
XLA Ops:
  0.0 31.9 %search.1 = f32[128,512]{1,0:T(8,128)} custom-call(s32[16,128]{1,0:T(8,128)} %bitcast.5, s32[14]{0:T(128)} %shift_hbm.1, bf16[1024,2048]{1,0:T(8,128)(2,1)} %bitcast.3, f32[256,512]{1,0:T(8,128)} %constant.2.clone.tables_hbm), custom_call_target="tpu_custom_call" | custom-call | tf_op jit(solution)/shard_map/search/pallas_call | solution.py:364
  32.0 1.7 %copy.6 = f32[8,2,8,512]{3,2,1,0:T(8,128)} copy(f32[8,2,8,512]{3,2,1,0:T(8,128)} %bitcast.4) | data formatting | bytes 524288

commit v2 on v1

--- a/solution.py
+++ b/solution.py
@@ -21,17 +21,17 @@
 SAMPLES = FRAMES * CHANS
 BANDS = CHANS // FSUM
 MEMBERS = 16
+SPLIT = 8
 LANES = 128
 MESH = pl.DeviceIdType.MESH
 
 
-def steer_tables():
+def steer_table():
     index = np.arange(NS)
     phase = (index[:, None] * index[None, :]) % NS
     angle = phase.astype(np.float32) * np.float32(2.0 * math.pi / NS)
-    order = [high * 16 + core * 8 + low for core in range(2) for high in range(16) for low in range(8)]
-    both = np.concatenate([np.cos(angle)[order], np.sin(angle)[order]], axis=1)
-    return jnp.asarray(both.astype(ml_dtypes.bfloat16).astype(np.float32))
+    table = np.concatenate([np.cos(angle)[: NS // 2 + 1], np.sin(angle)[1 : NS // 2]], axis=0)
+    return jnp.asarray(table.astype(ml_dtypes.bfloat16).astype(np.float32))
 
 
 def contract_last(left, right):
@@ -40,6 +40,19 @@
 
 def iota(shape, dim):
     return lax.broadcasted_iota(jnp.int32, shape, dim)
+
+
+def four_points(re, im):
+    even_re, even_im = re[0] + re[2], im[0] + im[2]
+    odd_re, odd_im = re[0] - re[2], im[0] - im[2]
+    side_re, side_im = re[1] + re[3], im[1] + im[3]
+    diff_re, diff_im = re[1] - re[3], im[1] - im[3]
+    return [
+        (even_re + side_re, even_im + side_im),
+        (odd_re + diff_im, odd_im - diff_re),
+        (even_re - side_re, even_im - side_im),
+        (odd_re - diff_im, odd_im + diff_re),
+    ]
 
 
 def swap_chunks(tiles):
@@ -59,18 +72,22 @@
 
 
 def search_kernel(
-    slot_hbm, shift_hbm, volt_hbm, tables_hbm, out_ref,
-    slot, owner_vmem, owner, shift_ref, volts, tables, turned, gridded, north,
+    slot_hbm, shift_hbm, volt_hbm, table_hbm, out_ref,
+    slot, owner_vmem, owner, shift_ref, volts, table, turned, gridded, north, power, highs, rests,
     own_ref, near, level_0, level_1, level_2, series, packed, landed, result,
     slot_sem, owner_sem, shift_sem, volt_sem, steer_sem,
     near_send, near_recv, far_send, far_recv, self_sem, out_sem,
 ):
     slot_copy = pltpu.make_async_copy(slot_hbm, slot, slot_sem)
-    steer_copy = pltpu.make_async_copy(tables_hbm, tables, steer_sem)
+    steer_copy = pltpu.make_async_copy(table_hbm, table, steer_sem)
     shift_copy = pltpu.make_async_copy(shift_hbm, shift_ref, shift_sem)
     volt_copies = [
-        pltpu.make_async_copy(volt_hbm.at[pl.ds(part * 256, 256)], volts.at[pl.ds(part * 256, 256)], volt_sem.at[part])
-        for part in range(4)
+        pltpu.make_async_copy(
+            volt_hbm.at[pl.ds(part * 1024 // SPLIT, 1024 // SPLIT)],
+            volts.at[pl.ds(part * 1024 // SPLIT, 1024 // SPLIT)],
+            volt_sem.at[part],
+        )
+        for part in range(SPLIT)
     ]
     for copy in [slot_copy] + volt_copies + [steer_copy, shift_copy]:
         copy.start()
@@ -118,88 +135,107 @@
     slot_copy.wait()
     places = iota((FEEDS // LANES, LANES), 0) * LANES + iota((FEEDS // LANES, LANES), 1)
     found = [jnp.zeros((FEEDS // LANES, LANES), jnp.int32) for _ in range(4)]
+    for feed in range(FEEDS):
+        found[feed % 4] = jnp.where(places == slot[feed // LANES, feed % LANES], feed, found[feed % 4])
+    owner_vmem[...] = jnp.maximum(jnp.maximum(found[0], found[1]), jnp.maximum(found[2], found[3]))
+    owner_copy = pltpu.make_async_copy(owner_vmem, owner, owner_sem)
+    owner_copy.start()
+
     for part in range(4):
-        volt_copies[part].wait()
-        rows = volts[pl.ds(part * 256, 256), :]
+        for piece in range(SPLIT // 4):
+            volt_copies[part * (SPLIT // 4) + piece].wait()
         for block in range(8):
-            flipped = jnp.transpose(rows[:, block * 256 : block * 256 + 256]).astype(jnp.float32)
+            flipped = jnp.transpose(volts[pl.ds(part * 256, 256), block * 256 : block * 256 + 256]).astype(jnp.float32)
             for half_rows in range(2):
                 turned[pl.ds(block * 2048 + part * 2 + half_rows, 256, stride=8), :] = flipped[
                     :, half_rows * LANES : half_rows * LANES + LANES
                 ]
-            if part < 2:
-                row = part * 8 + block
-                for lane in range(LANES):
-                    found[lane % 4] = jnp.where(places == slot[row, lane], row * LANES + lane, found[lane % 4])
-        if part == 1:
-            owner_vmem[...] = jnp.maximum(jnp.maximum(found[0], found[1]), jnp.maximum(found[2], found[3]))
-            owner_copy = pltpu.make_async_copy(owner_vmem, owner, owner_sem)
-            owner_copy.start()
-
+
+    steer_copy.wait()
+    steer = table[...].astype(jnp.bfloat16)
     owner_copy.wait()
-
-    def move(row, carry):
-        for lane in range(LANES):
-            feed = owner[row, lane]
-            first = pl.multiple_of((row * LANES + lane) * 8, 8)
-            gridded[pl.ds(first, 8), :] = turned[pl.ds(feed * 8, 8), :]
-        return carry
-
-    lax.fori_loop(0, FEEDS // LANES, move, 0)
-
-    steer_copy.wait()
-    top = tables[...].astype(jnp.bfloat16)
-    steer = jnp.concatenate([top, jnp.concatenate([-top[:, NS:], top[:, :NS]], axis=1)], axis=0)
-    for pol in range(POL):
-        for cyl in range(EW):
-            first = (pol * EW + cyl) * NS * 8
-            parts = [gridded[pl.ds(first + q, NS, stride=8), :].astype(jnp.bfloat16) for q in range(8)]
-            both = jnp.concatenate(
-                [jnp.concatenate(parts[:4], axis=1), jnp.concatenate(parts[4:], axis=1)], axis=0
+    def gather(branch):
+        for place in range(NS):
+            at = branch * NS + place
+            feed = owner[at // LANES, at % LANES]
+            gridded[branch][pl.ds(place * 8, 8), :] = turned[pl.ds(feed * 8, 8), :]
+
+    def transform(branch):
+        data = [gridded[branch][pl.ds(q, NS, stride=8), :].astype(jnp.bfloat16) for q in range(8)]
+        north[branch] = jnp.dot(steer, jnp.concatenate(data, axis=1), preferred_element_type=jnp.float32)
+
+    first_row = iota((16, LANES), 0) == 0
+
+    def energy(pol, strip):
+        plus_rows, minus_rows = slice(strip * 16, strip * 16 + 16), slice(128 + strip * 16, 144 + strip * 16)
+        for chunk in range(4):
+            reals, imags = slice(chunk * LANES, chunk * LANES + LANES), slice(512 + chunk * LANES, 640 + chunk * LANES)
+            at = pol * EW
+            even = four_points(
+                [north[at + e, plus_rows, reals] for e in range(EW)],
+                [north[at + e, plus_rows, imags] for e in range(EW)],
             )
-            north[pol * EW + cyl] = jnp.dot(steer, both, preferred_element_type=jnp.float32)
-
-    bin_row, sample = iota((BANDS * FRAMES, SAMPLES), 0), iota((BANDS * FRAMES, SAMPLES), 1)
-    chosen = (sample // CHANS == bin_row % FRAMES) & (sample % CHANS // FSUM == bin_row // FRAMES)
-    adder = jnp.where(chosen, 0.5 / FEEDS, 0.0).astype(jnp.bfloat16)
-    binned = [[] for _ in range(EW)]
-    for strip in range(2):
-        energies = [[] for _ in range(EW)]
-        for piece in range(8):
-            top = pl.ds(strip * 128 + piece * 16, 16)
-            low = pl.ds(NS + strip * 128 + piece * 16, 16)
-            power = [None] * EW
-            for pol in range(POL):
-                re = [north[pol * EW + cyl, top, :] for cyl in range(EW)]
-                im = [north[pol * EW + cyl, low, :] for cyl in range(EW)]
-                even_re, even_im = re[0] + re[2], im[0] + im[2]
-                odd_re, odd_im = re[0] - re[2], im[0] - im[2]
-                side_re, side_im = re[1] + re[3], im[1] + im[3]
-                diff_re, diff_im = re[1] - re[3], im[1] - im[3]
-                sums = [
-                    (even_re + side_re, even_im + side_im),
-                    (odd_re + diff_im, odd_im - diff_re),
-                    (even_re - side_re, even_im - side_im),
-                    (odd_re - diff_im, odd_im + diff_re),
-                ]
-                for column in range(EW):
-                    energy = sums[column][0] * sums[column][0] + sums[column][1] * sums[column][1]
-                    power[column] = energy if pol == 0 else power[column] + energy
+            odd = four_points(
+                [north[at + e, minus_rows, reals] for e in range(EW)],
+                [north[at + e, minus_rows, imags] for e in range(EW)],
+            )
             for column in range(EW):
-                energies[column].append(power[column])
-        for column in range(EW):
-            whole = jnp.concatenate(energies[column], axis=0)
-            high = whole.astype(jnp.bfloat16)
-            rest = (whole - high.astype(jnp.float32)).astype(jnp.bfloat16)
-            binned[column].append(contract_last(adder, high) + contract_last(adder, rest))
+                (even_re, even_im), (odd_re, odd_im) = even[column], odd[column]
+                plus_re, plus_im = even_re + odd_im, even_im - odd_re
+                minus_re, minus_im = even_re - odd_im, even_im + odd_re
+                if strip == 0:
+                    plus_re, plus_im = jnp.where(first_row, even_re, plus_re), jnp.where(first_row, even_im, plus_im)
+                    minus_re, minus_im = jnp.where(first_row, odd_re, minus_re), jnp.where(first_row, odd_im, minus_im)
+                plus = plus_re * plus_re + plus_im * plus_im
+                minus = minus_re * minus_re + minus_im * minus_im
+                for first, part in ((strip * 32, plus), (strip * 32 + 16, minus)):
+                    rows = slice(first, first + 16)
+                    if pol == 0:
+                        power[column, rows, reals] = part
+                    else:
+                        part = part + power[column, rows, reals]
+                        high = part.astype(jnp.bfloat16)
+                        highs[column, rows, reals] = high
+                        rests[column, rows, reals] = (part - high.astype(jnp.float32)).astype(jnp.bfloat16)
+
+    gather(0)
+    for branch in range(POL * EW):
+        if branch + 1 < POL * EW:
+            gather(branch + 1)
+        transform(branch)
+        if branch >= EW:
+            energy(0, 2 * (branch - EW))
+            energy(0, 2 * (branch - EW) + 1)
+
+    for strip in range(8):
+        energy(1, strip)
+    sample, place = iota((SAMPLES, LANES), 0), iota((SAMPLES, LANES), 1)
+    chosen = (sample // CHANS == place % FRAMES) & (sample % CHANS // FSUM == place // FRAMES % BANDS)
+    sums = jnp.zeros((NS, LANES), jnp.float32)
+    for column in range(EW):
+        own = chosen & (place // (BANDS * FRAMES) == column)
+        adder = jnp.where(own, 0.5 / FEEDS, 0.0).astype(jnp.bfloat16)
+        sums = sums + jnp.dot(highs[column], adder, preferred_element_type=jnp.float32)
+        sums = sums + jnp.dot(rests[column], adder, preferred_element_type=jnp.float32)
+    lane, source = iota((NS, NS), 1), iota((NS, NS), 0)
+    output = lane // 8 % 16 * 16 + lane // 128 * 8 + lane % 8
+    folded = jnp.where(output < 128, output, (256 - output) % 128)
+    home = folded // 16 * 32 + folded % 16 + jnp.where(output < 128, 0, 16)
+    order = jnp.where(source == home, 1.0, 0.0).astype(jnp.bfloat16)
     low_lanes = iota((16, LANES), 1) < LANES // 2
+    binned = jnp.transpose(sums)
+    high = binned.astype(jnp.bfloat16)
+    rest = (binned - high.astype(jnp.float32)).astype(jnp.bfloat16)
+    binned = jnp.dot(high, order, preferred_element_type=jnp.float32) + jnp.dot(
+        rest, order, preferred_element_type=jnp.float32
+    )
     for column in range(EW):
         for c in range(2):
-            one, two = binned[column][c][0:16], binned[column][c][16:32]
+            lanes = slice(c * LANES, c * LANES + LANES)
+            one, two = binned[column * 32 : column * 32 + 16, lanes], binned[column * 32 + 16 : column * 32 + 32, lanes]
             target = (c * 2 + column // 2) * 4 + column % 2 * 2
             own_ref[target] = jnp.where(low_lanes, one, pltpu.roll(two, LANES // 2, 1))
             own_ref[target + 1] = jnp.where(low_lanes, pltpu.roll(one, LANES // 2, 1), two)
-
 
     pl.semaphore_wait(barrier, jnp.where(selfish, MEMBERS + 14, MEMBERS + 15))
 
@@ -372,10 +408,13 @@
             pltpu.SMEM((FEEDS // LANES, LANES), jnp.int32),
             pltpu.SMEM((14,), jnp.int32),
             pltpu.VMEM((2 * SAMPLES, FEEDS), jnp.bfloat16),
-            pltpu.VMEM((NS, 2 * NS), jnp.float32),
+            pltpu.VMEM((NS, NS), jnp.float32),
             pltpu.VMEM((FEEDS * 8, LANES), jnp.float32),
-            pltpu.VMEM((FEEDS * 8, LANES), jnp.float32),
-            pltpu.VMEM((POL * EW, 2 * NS, SAMPLES), jnp.float32),
+            [pltpu.VMEM((NS * 8, LANES), jnp.float32)] * (POL * EW),
+            pltpu.VMEM((POL * EW, NS, 2 * SAMPLES), jnp.float32),
+            pltpu.VMEM((EW, NS, SAMPLES), jnp.float32),
+            pltpu.VMEM((EW, NS, SAMPLES), jnp.bfloat16),
+            pltpu.VMEM((EW, NS, SAMPLES), jnp.bfloat16),
             pltpu.VMEM((MEMBERS, 16, LANES), jnp.float32),
             pltpu.VMEM((MEMBERS, 16, LANES), jnp.float32),
             level,
@@ -388,7 +427,7 @@
             dma,
             dma,
             dma,
-            dma((4,)),
+            dma((SPLIT,)),
             dma,
             dma,
             dma,
@@ -405,7 +444,7 @@
         feed_slot.reshape(FEEDS // LANES, LANES),
         tree_shift,
         voltages.reshape(2 * SAMPLES, FEEDS),
-        steer_tables(),
+        steer_table(),
     )
 
 

time: 34 us -> 33.1 us (0.974)
  Pallas kernels: 31.9 us -> 31 us
    pallas_call x1, Pallas kernels: 31.9 us -> 31 us  [search(): pl.pallas_call(search_kernel, out_shape=jax.ShapeDtypeStruct((8 * BOXES *...]
where the time goes in v2:
time: 33.1 us; the launch traced here: 32.7 us
  Pallas kernels  31 us (94%)
  local copies, waits for them, and re-layouts  1.67 us (5%)
    pallas_call x1, Pallas kernels, search(): pl.pallas_call(search_kernel, out_shape=jax.ShapeDtypeStruct((8 * BOXES *...  31 us
    unnamed x1, local copies, waits for them, and re-layouts  1.67 us

profile of v2, /device:TPU:1, one launch (start us, length us, event | category | flops | bytes accessed | tf_op | source)
XLA Modules:
  0.0 32.7 jit_solution(8268527707729006617)
XLA Ops:
  0.0 31.0 %search.1 = f32[128,512]{1,0:T(8,128)} custom-call(s32[16,128]{1,0:T(8,128)} %bitcast.5, s32[14]{0:T(128)} %shift_hbm.1, bf16[1024,2048]{1,0:T(8,128)(2,1)} %bitcast.3, f32[256,256]{1,0:T(8,128)} %constant.2.clone.table_hbm), custom_call_target="tpu_custom_call" | custom-call | tf_op jit(solution)/shard_map/search/pallas_call | solution.py:400
  31.0 1.7 %copy.6 = f32[8,2,8,512]{3,2,1,0:T(8,128)} copy(f32[8,2,8,512]{3,2,1,0:T(8,128)} %bitcast.4) | data formatting | bytes 524288

commit v3 on v2

--- a/solution.py
+++ b/solution.py
@@ -1,3 +1,4 @@
+import itertools
 import math
 
 import jax
@@ -72,11 +73,11 @@
 
 
 def search_kernel(
-    slot_hbm, shift_hbm, volt_hbm, table_hbm, out_ref,
+    slot_hbm, shift_hbm, volt_hbm, table_hbm, landed,
     slot, owner_vmem, owner, shift_ref, volts, table, turned, gridded, north, power, highs, rests,
-    own_ref, near, level_0, level_1, level_2, series, packed, landed, result,
+    own_ref, near, level_0, level_1, level_2, series, early, late,
     slot_sem, owner_sem, shift_sem, volt_sem, steer_sem,
-    near_send, near_recv, far_send, far_recv, self_sem, out_sem,
+    near_send, near_recv, far_send, far_recv, self_sem,
 ):
     slot_copy = pltpu.make_async_copy(slot_hbm, slot, slot_sem)
     steer_copy = pltpu.make_async_copy(table_hbm, table, steer_sem)
@@ -92,7 +93,6 @@
     for copy in [slot_copy] + volt_copies + [steer_copy, shift_copy]:
         copy.start()
 
-    landed[:, :, 4:8, :] = jnp.zeros((16, 4, 4, LANES), jnp.float32)
     for buffer in (level_0, level_1, level_2):
         buffer[:, :, 16:24, :] = jnp.zeros((2, 8, 8, LANES), jnp.float32)
     place = lax.axis_index("beam")
@@ -249,11 +249,9 @@
             device_id_type=MESH,
         )
 
-    def send_near(step, carry):
-        near_copy(lax.rem(member + step, MEMBERS)).start()
-        return carry
-
-    lax.fori_loop(1, MEMBERS, send_near, 0)
+    for dy, dx, dc in itertools.product((2, 1, 3, 0), (1, 0), (1, 0)):
+        if dy + dx + dc > 0:
+            near_copy((lax.rem(core + dc, 2) * 2 + lax.rem(half + dx, 2)) * 4 + lax.rem(y + dy, 4)).start()
     mine = pltpu.make_async_copy(own_ref.at[member], near.at[member], self_sem)
     mine.start()
     mine.wait()
@@ -287,22 +285,30 @@
                     buffers[level + 1][pair, band, 0:16, :] = total
                 else:
                     series[pair, pl.ds(band, 16, stride=8), :] = total
-    keep = (iota((8, LANES), 1) < LANES // 2) == (iota((8, LANES), 0) < 4)
+    low_half = iota((8, LANES), 1) < LANES // 2
+    low_rows = iota((8, LANES), 0) < 4
+    chunk = iota((8, LANES), 1) // 8
+    ninth = [jnp.zeros((8, LANES), jnp.float32) for _ in range(8)]
     for pair in range(2):
         flipped = jnp.transpose(series[pair])
-        for low in range(2):
-            for target in range(8):
-                first = low * 64 + target * 8
-                tile = flipped[first : first + 8]
+        for target in range(8):
+            for low in range(2):
+                tile = flipped[low * 64 + target * 8 : low * 64 + target * 8 + 8]
+                at = pair * 2 + low
                 crossed = pltpu.roll(pltpu.roll(tile, 4, 0), LANES // 2, 1)
-                packed[target, pair * 2 + low] = jnp.where(keep, tile, crossed)
-
-    slot = x_high * 8 + z
+                both = jnp.where(low_half == low_rows, tile, crossed)
+                early[target, at * 4 : at * 4 + 4, :] = both[0:4]
+                late[target, at * 4 : at * 4 + 4, :] = both[4:8]
+                ninth[target] = jnp.where(chunk == at, pltpu.roll(tile, LANES // 2 + at * 8, 1), ninth[target])
+    for target in range(8):
+        early[target, 16:24, :] = ninth[target]
+
+    source = x_high * 8 + z
 
     def to_early(target):
         return pltpu.make_async_remote_copy(
-            src_ref=packed.at[target],
-            dst_ref=landed.at[slot],
+            src_ref=early.at[target],
+            dst_ref=landed.at[source],
             send_sem=far_send.at[0],
             recv_sem=far_recv,
             device_id=at_site(half, target, 0),
@@ -311,8 +317,8 @@
 
     def to_late(target):
         return pltpu.make_async_remote_copy(
-            src_ref=packed.at[target, :, 4:8],
-            dst_ref=landed.at[slot, :, 0:4],
+            src_ref=late.at[target],
+            dst_ref=landed.at[source, 0:16],
             send_sem=far_send.at[1],
             recv_sem=far_recv,
             device_id=at_site(half, target, 1),
@@ -321,77 +327,113 @@
 
     early_self = jnp.logical_and(selfish, half == 0)
     late_self = jnp.logical_and(selfish, half == 1)
-
-    def send(step, carry):
-        target = lax.rem(z + step, 8)
-
-        @pl.when(jnp.logical_not(jnp.logical_and(target == z, early_self)))
-        def _():
-            to_early(target).start()
-
-        @pl.when(jnp.logical_not(jnp.logical_and(target == z, late_self)))
-        def _():
-            to_late(target).start()
-
-        return carry
-
-    lax.fori_loop(0, 8, send, 0)
+    for dz in (4, 3, 5, 2, 6, 1, 7):
+        to_early(lax.rem(z + dz, 8)).start()
+        to_late(lax.rem(z + dz, 8)).start()
+
+    @pl.when(jnp.logical_not(early_self))
+    def _():
+        to_early(z).start()
+
+    @pl.when(jnp.logical_not(late_self))
+    def _():
+        to_late(z).start()
 
     @pl.when(early_self)
     def _():
-        copy = pltpu.make_async_copy(packed.at[z], landed.at[slot], self_sem)
+        copy = pltpu.make_async_copy(early.at[z], landed.at[source], self_sem)
         copy.start()
         copy.wait()
 
     @pl.when(late_self)
     def _():
-        copy = pltpu.make_async_copy(packed.at[z, :, 4:8], landed.at[slot, :, 0:4], self_sem)
+        copy = pltpu.make_async_copy(late.at[z], landed.at[source, 0:16], self_sem)
         copy.start()
         copy.wait()
 
-    def wait_for(buffer, sem, count, rows):
-        part = buffer.at[0:count, :, 0:rows]
+    def wait_for(part, sem):
         pltpu.make_async_copy(part, part, sem).wait()
 
-    for h, rows in ((0, 8), (1, 4)):
+    for h, rows in ((0, 24), (1, 16)):
         @pl.when(jnp.logical_and(half == h, selfish))
         def _():
-            wait_for(landed, far_recv, 15, rows)
+            wait_for(landed.at[0:15, 0:rows], far_recv)
 
         @pl.when(jnp.logical_and(half == h, jnp.logical_not(selfish)))
         def _():
-            wait_for(landed, far_recv, 16, rows)
-
-    writes = []
-    for block in range(4):
-        xx, pair = block // 2, block % 2
-        tiles = swap_chunks([landed[xx * 8 + zz, pair * 2 + low] for low in range(2) for zz in range(8)])
-        for high in range(2):
-            for frame in range(8):
-                now = tiles[high * 8 + frame]
-                if frame < 7:
-                    later = tiles[high * 8 + frame + 1]
-                else:
-                    later = pltpu.roll(tiles[high * 8], 4, 0)
-                first = high * 64 + frame
-                result[block, pl.ds(first, 4, stride=16), :] = (now * (1.0 / (FSUM * 8)))[0:4]
-                result[block, pl.ds(first + 8, 4, stride=16), :] = ((now + later) * (1.0 / (FSUM * 16)))[0:4]
-        write = pltpu.make_async_copy(result.at[block], out_ref.at[:, pl.ds(block * LANES, LANES)], out_sem.at[block])
-        write.start()
-        writes.append(write)
-
-    pltpu.make_async_copy(own_ref.at[0:15], own_ref.at[0:15], near_send).wait()
-    for flag, index, rows in ((early_self, 0, 8), (late_self, 1, 4)):
+            wait_for(landed.at[:, 0:rows], far_recv)
+
+    wait_for(own_ref.at[0:15], near_send)
+    for flag, index, buffer in ((early_self, 0, early), (late_self, 1, late)):
         @pl.when(flag)
         def _():
-            wait_for(packed, far_send.at[index], 7, rows)
+            wait_for(buffer.at[0:7], far_send.at[index])
 
         @pl.when(jnp.logical_not(flag))
         def _():
-            wait_for(packed, far_send.at[index], 8, rows)
-
+            wait_for(buffer, far_send.at[index])
+
+
+def finish_kernel(landed_hbm, out_ref, landed, result, in_sem, out_sem):
+    reads = [
+        pltpu.make_async_copy(landed_hbm.at[xx * 8 : xx * 8 + 8], landed.at[xx * 8 : xx * 8 + 8], in_sem.at[xx])
+        for xx in range(2)
+    ]
+    for copy in reads:
+        copy.start()
+    chunk = iota((8, LANES), 1) // 8
+    has_ninth = jnp.broadcast_to(lax.axis_index("tm"), (8, LANES)) == 0
+    writes = []
+    for xx in range(2):
+        reads[xx].wait()
+        for pair in range(2):
+            block = xx * 2 + pair
+            tiles = []
+            ninth = jnp.zeros((8, LANES), jnp.float32)
+            for low in range(2):
+                at = pair * 2 + low
+                for zz in range(8):
+                    tiles.append(landed[xx * 8 + zz, at * 4 : at * 4 + 8, :])
+                    to = low * 8 + zz
+                    ninth = jnp.where(
+                        chunk == to, pltpu.roll(landed[xx * 8 + zz, 16:24, :], (to - at) * 8 % LANES, 1), ninth
+                    )
+            ninth = jnp.where(has_ninth, ninth, 0.0)
+            tiles = swap_chunks(tiles)
+            for high in range(2):
+                for frame in range(8):
+                    now = tiles[high * 8 + frame][0:4]
+                    if frame < 7:
+                        later = tiles[high * 8 + frame + 1][0:4]
+                    else:
+                        later = ninth[high * 4 : high * 4 + 4]
+                    first = high * 64 + frame
+                    result[block, pl.ds(first, 4, stride=16), :] = now * (1.0 / (FSUM * 8))
+                    result[block, pl.ds(first + 8, 4, stride=16), :] = (now + later) * (1.0 / (FSUM * 16))
+            write = pltpu.make_async_copy(
+                result.at[block], out_ref.at[:, pl.ds(block * LANES, LANES)], out_sem.at[block]
+            )
+            write.start()
+            writes.append(write)
     for write in writes:
         write.wait()
+
+
+def finish(landed):
+    return pl.pallas_call(
+        finish_kernel,
+        out_shape=jax.ShapeDtypeStruct((8 * BOXES * FRAMES, 512), jnp.float32),
+        in_specs=[pl.BlockSpec(memory_space=pltpu.HBM)],
+        out_specs=pl.BlockSpec(memory_space=pltpu.HBM),
+        scratch_shapes=[
+            pltpu.VMEM((16, 24, LANES), jnp.float32),
+            pltpu.VMEM((4, 128, LANES), jnp.float32),
+            pltpu.SemaphoreType.DMA((2,)),
+            pltpu.SemaphoreType.DMA((4,)),
+        ],
+        compiler_params=pltpu.CompilerParams(vmem_limit_bytes=60 * 2**20),
+        name="finish",
+    )(landed)
 
 
 def search(voltages, feed_slot, tree_shift):
@@ -399,9 +441,9 @@
     dma = pltpu.SemaphoreType.DMA
     return pl.pallas_call(
         search_kernel,
-        out_shape=jax.ShapeDtypeStruct((8 * BOXES * FRAMES, 512), jnp.float32),
+        out_shape=jax.ShapeDtypeStruct((16, 24, LANES), jnp.float32),
         in_specs=[pl.BlockSpec(memory_space=pltpu.HBM)] * 4,
-        out_specs=pl.BlockSpec(memory_space=pl.ANY),
+        out_specs=pl.BlockSpec(memory_space=pltpu.HBM),
         scratch_shapes=[
             pltpu.SMEM((FEEDS // LANES, LANES), jnp.int32),
             pltpu.VMEM((FEEDS // LANES, LANES), jnp.int32),
@@ -421,9 +463,8 @@
             level,
             level,
             pltpu.VMEM((2, 128, LANES), jnp.float32),
-            pltpu.VMEM((8, 4, 8, LANES), jnp.float32),
-            pltpu.VMEM((16, 4, 8, LANES), jnp.float32),
-            pltpu.VMEM((4, 128, LANES), jnp.float32),
+            pltpu.VMEM((8, 24, LANES), jnp.float32),
+            pltpu.VMEM((8, 16, LANES), jnp.float32),
             dma,
             dma,
             dma,
@@ -434,7 +475,6 @@
             dma((2,)),
             dma,
             dma,
-            dma((4,)),
         ],
         compiler_params=pltpu.CompilerParams(
             collective_id=0, has_side_effects=True, vmem_limit_bytes=60 * 2**20
@@ -449,7 +489,7 @@
 
 
 def on_device(voltages, feed_slot, tree_shift):
-    result = search(voltages, feed_slot, tree_shift)
+    result = finish(search(voltages, feed_slot, tree_shift))
     return result.reshape(8, BOXES, FRAMES, 512)
 
 

time: 33.1 us -> 31.6 us (0.955); the launches traced: 32.7 us -> 31.5 us
  local copies, waits for them, and re-layouts: 1.67 us -> 0 us
  Pallas kernels: 31 us -> 31.5 us
    unnamed x1 -> x0, local copies, waits for them, and re-layouts: 1.67 us -> none
    pallas_call x1 -> x2, Pallas kernels: 31 us -> 31.5 us  [the longest x1 29.3 us: search(): pl.pallas_call(search_kernel, out_shape=jax.ShapeDtypeStruct((16, 24, LAN...]
where the time goes in v3:
time: 31.6 us; the launch traced here: 31.5 us
  Pallas kernels  31.5 us (100%)
    pallas_call x1, Pallas kernels, search(): pl.pallas_call(search_kernel, out_shape=jax.ShapeDtypeStruct((16, 24, LAN...  29.3 us
    pallas_call x1, Pallas kernels, finish(): pl.pallas_call(finish_kernel, out_shape=jax.ShapeDtypeStruct((8 * BOXES *...  2.27 us

profile of v3, /device:TPU:1, one launch (start us, length us, event | category | flops | bytes accessed | tf_op | source)
XLA Modules:
  0.0 31.5 jit_solution(12130971922265615383)
XLA Ops:
  0.0 29.3 %search.1.landed_hbm = f32[16,24,128]{2,1,0:T(8,128)} custom-call(s32[16,128]{1,0:T(8,128)} %bitcast.4, s32[14]{0:T(128)} %shift_hbm.1, bf16[1024,2048]{1,0:T(8,128)(2,1)} %bitcast.3, f32[256,256]{1,0:T(8,128)} %constant.2.clone.table_hbm), custom_call_target="tpu_custom_call" | custom-call | tf_op jit(solution)/shard_map/search/pallas_call | solution.py:442
  29.3 2.3 %finish.1 = f32[128,512]{1,0:T(8,128)} custom-call(f32[16,24,128]{2,1,0:T(8,128)} %search.1.landed_hbm), custom_call_target="tpu_custom_call" | custom-call | tf_op jit(solution)/shard_map/finish/pallas_call | solution.py:423

commit v4 on v3

--- a/solution.py
+++ b/solution.py
@@ -374,18 +374,11 @@
             wait_for(buffer, far_send.at[index])
 
 
-def finish_kernel(landed_hbm, out_ref, landed, result, in_sem, out_sem):
-    reads = [
-        pltpu.make_async_copy(landed_hbm.at[xx * 8 : xx * 8 + 8], landed.at[xx * 8 : xx * 8 + 8], in_sem.at[xx])
-        for xx in range(2)
-    ]
-    for copy in reads:
-        copy.start()
+def finish_kernel(landed, out_ref, result, out_sem):
     chunk = iota((8, LANES), 1) // 8
     has_ninth = jnp.broadcast_to(lax.axis_index("tm"), (8, LANES)) == 0
     writes = []
     for xx in range(2):
-        reads[xx].wait()
         for pair in range(2):
             block = xx * 2 + pair
             tiles = []
@@ -422,16 +415,14 @@
 def finish(landed):
     return pl.pallas_call(
         finish_kernel,
-        out_shape=jax.ShapeDtypeStruct((8 * BOXES * FRAMES, 512), jnp.float32),
-        in_specs=[pl.BlockSpec(memory_space=pltpu.HBM)],
+        out_shape=pltpu.HBM((8 * BOXES * FRAMES, 512), jnp.float32),
+        in_specs=[pl.BlockSpec(memory_space=pltpu.VMEM)],
         out_specs=pl.BlockSpec(memory_space=pltpu.HBM),
         scratch_shapes=[
-            pltpu.VMEM((16, 24, LANES), jnp.float32),
             pltpu.VMEM((4, 128, LANES), jnp.float32),
-            pltpu.SemaphoreType.DMA((2,)),
             pltpu.SemaphoreType.DMA((4,)),
         ],
-        compiler_params=pltpu.CompilerParams(vmem_limit_bytes=60 * 2**20),
+        compiler_params=pltpu.CompilerParams(vmem_limit_bytes=16 * 2**20),
         name="finish",
     )(landed)
 
@@ -441,9 +432,9 @@
     dma = pltpu.SemaphoreType.DMA
     return pl.pallas_call(
         search_kernel,
-        out_shape=jax.ShapeDtypeStruct((16, 24, LANES), jnp.float32),
+        out_shape=pltpu.VMEM((16, 24, LANES), jnp.float32),
         in_specs=[pl.BlockSpec(memory_space=pltpu.HBM)] * 4,
-        out_specs=pl.BlockSpec(memory_space=pltpu.HBM),
+        out_specs=pl.BlockSpec(memory_space=pltpu.VMEM),
         scratch_shapes=[
             pltpu.SMEM((FEEDS // LANES, LANES), jnp.int32),
             pltpu.VMEM((FEEDS // LANES, LANES), jnp.int32),

time: 31.6 us -> 30.4 us (0.962)
  Pallas kernels: 31.5 us -> 30.3 us
    pallas_call x2, Pallas kernels: 31.5 us -> 30.3 us  [the longest x1 29 us: search(): pl.pallas_call(search_kernel, out_shape=pltpu.VMEM((16, 24, LANES), jnp.f...]
where the time goes in v4:
time: 30.4 us; the launch traced here: 30.3 us
  Pallas kernels  30.3 us (100%)
    pallas_call x1, Pallas kernels, search(): pl.pallas_call(search_kernel, out_shape=pltpu.VMEM((16, 24, LANES), jnp.f...  29 us
    pallas_call x1, Pallas kernels, finish(): pl.pallas_call(finish_kernel, out_shape=pltpu.HBM((8 * BOXES * FRAMES, 51...  1.29 us

profile of v4, /device:TPU:1, one launch (start us, length us, event | category | flops | bytes accessed | tf_op | source)
XLA Modules:
  0.0 30.3 jit_solution(6220120939949167287)
XLA Ops:
  0.0 29.0 %search.1.landed = f32[16,24,128]{2,1,0:T(8,128)S(1)} custom-call(s32[16,128]{1,0:T(8,128)} %bitcast.4, s32[14]{0:T(128)} %shift_hbm.1, bf16[1024,2048]{1,0:T(8,128)(2,1)} %bitcast.3, f32[256,256]{1,0:T(8,128)} %constant.2.clone.table_hbm), custom_call_target="tpu_custom_call" | custom-call | tf_op jit(solution)/shard_map/search/pallas_call | solution.py:433
  29.0 1.3 %finish.1 = f32[128,512]{1,0:T(8,128)} custom-call(f32[16,24,128]{2,1,0:T(8,128)S(1)} %search.1.landed), custom_call_target="tpu_custom_call" | custom-call | tf_op jit(solution)/shard_map/finish/pallas_call | solution.py:416

commit v5 on v4

--- a/solution.py
+++ b/solution.py
@@ -22,7 +22,7 @@
 SAMPLES = FRAMES * CHANS
 BANDS = CHANS // FSUM
 MEMBERS = 16
-SPLIT = 8
+SPLIT = 4
 LANES = 128
 MESH = pl.DeviceIdType.MESH
 
@@ -164,12 +164,12 @@
         data = [gridded[branch][pl.ds(q, NS, stride=8), :].astype(jnp.bfloat16) for q in range(8)]
         north[branch] = jnp.dot(steer, jnp.concatenate(data, axis=1), preferred_element_type=jnp.float32)
 
-    first_row = iota((16, LANES), 0) == 0
+    first_row = iota((16, 256), 0) == 0
 
     def energy(pol, strip):
         plus_rows, minus_rows = slice(strip * 16, strip * 16 + 16), slice(128 + strip * 16, 144 + strip * 16)
-        for chunk in range(4):
-            reals, imags = slice(chunk * LANES, chunk * LANES + LANES), slice(512 + chunk * LANES, 640 + chunk * LANES)
+        for chunk in range(2):
+            reals, imags = slice(chunk * 256, chunk * 256 + 256), slice(512 + chunk * 256, 768 + chunk * 256)
             at = pol * EW
             even = four_points(
                 [north[at + e, plus_rows, reals] for e in range(EW)],
@@ -203,11 +203,9 @@
         if branch + 1 < POL * EW:
             gather(branch + 1)
         transform(branch)
-        if branch >= EW:
-            energy(0, 2 * (branch - EW))
-            energy(0, 2 * (branch - EW) + 1)
 
     for strip in range(8):
+        energy(0, strip)
         energy(1, strip)
     sample, place = iota((SAMPLES, LANES), 0), iota((SAMPLES, LANES), 1)
     chosen = (sample // CHANS == place % FRAMES) & (sample % CHANS // FSUM == place // FRAMES % BANDS)

time: 30.4 us -> 30 us (0.987)
    pallas_call x1, Pallas kernels: 29 us -> 28.7 us  [search(): pl.pallas_call(search_kernel, out_shape=pltpu.VMEM((16, 24, LANES), jnp.f...]
where the time goes in v5:
time: 30 us
  Pallas kernels  30 us (100%)
    pallas_call x1, Pallas kernels, search(): pl.pallas_call(search_kernel, out_shape=pltpu.VMEM((16, 24, LANES), jnp.f...  28.7 us
    pallas_call x1, Pallas kernels, finish(): pl.pallas_call(finish_kernel, out_shape=pltpu.HBM((8 * BOXES * FRAMES, 51...  1.29 us

profile of v5, /device:TPU:1, one launch (start us, length us, event | category | flops | bytes accessed | tf_op | source)
XLA Modules:
  0.0 30.0 jit_solution(5721081690858672291)
XLA Ops:
  0.0 28.7 %search.1.landed = f32[16,24,128]{2,1,0:T(8,128)S(1)} custom-call(s32[16,128]{1,0:T(8,128)} %bitcast.4, s32[14]{0:T(128)} %shift_hbm.1, bf16[1024,2048]{1,0:T(8,128)(2,1)} %bitcast.3, f32[256,256]{1,0:T(8,128)} %constant.2.clone.table_hbm), custom_call_target="tpu_custom_call" | custom-call | tf_op jit(solution)/shard_map/search/pallas_call | solution.py:431
  28.7 1.3 %finish.1 = f32[128,512]{1,0:T(8,128)} custom-call(f32[16,24,128]{2,1,0:T(8,128)S(1)} %search.1.landed), custom_call_target="tpu_custom_call" | custom-call | tf_op jit(solution)/shard_map/finish/pallas_call | solution.py:414

commit v6 on v5

--- a/solution.py
+++ b/solution.py
@@ -164,12 +164,12 @@
         data = [gridded[branch][pl.ds(q, NS, stride=8), :].astype(jnp.bfloat16) for q in range(8)]
         north[branch] = jnp.dot(steer, jnp.concatenate(data, axis=1), preferred_element_type=jnp.float32)
 
-    first_row = iota((16, 256), 0) == 0
+    first_row = iota((16, SAMPLES), 0) == 0
 
     def energy(pol, strip):
         plus_rows, minus_rows = slice(strip * 16, strip * 16 + 16), slice(128 + strip * 16, 144 + strip * 16)
-        for chunk in range(2):
-            reals, imags = slice(chunk * 256, chunk * 256 + 256), slice(512 + chunk * 256, 768 + chunk * 256)
+        for chunk in range(1):
+            reals, imags = slice(0, SAMPLES), slice(SAMPLES, 2 * SAMPLES)
             at = pol * EW
             even = four_points(
                 [north[at + e, plus_rows, reals] for e in range(EW)],

time: 30 us -> 30.1 us (level)
  no operation moved by 1% of the time
where the time goes in v6:
time: 30.1 us; the launch traced here: 30 us
  Pallas kernels  30 us (100%)
    pallas_call x1, Pallas kernels, search(): pl.pallas_call(search_kernel, out_shape=pltpu.VMEM((16, 24, LANES), jnp.f...  28.7 us
    pallas_call x1, Pallas kernels, finish(): pl.pallas_call(finish_kernel, out_shape=pltpu.HBM((8 * BOXES * FRAMES, 51...  1.29 us

profile of v6, /device:TPU:1, one launch (start us, length us, event | category | flops | bytes accessed | tf_op | source)
XLA Modules:
  0.0 30.0 jit_solution(5721081690858672291)
XLA Ops:
  0.0 28.7 %search.1.landed = f32[16,24,128]{2,1,0:T(8,128)S(1)} custom-call(s32[16,128]{1,0:T(8,128)} %bitcast.4, s32[14]{0:T(128)} %shift_hbm.1, bf16[1024,2048]{1,0:T(8,128)(2,1)} %bitcast.3, f32[256,256]{1,0:T(8,128)} %constant.2.clone.table_hbm), custom_call_target="tpu_custom_call" | custom-call | tf_op jit(solution)/shard_map/search/pallas_call | solution.py:431
  28.7 1.3 %finish.1 = f32[128,512]{1,0:T(8,128)} custom-call(f32[16,24,128]{2,1,0:T(8,128)S(1)} %search.1.landed), custom_call_target="tpu_custom_call" | custom-call | tf_op jit(solution)/shard_map/finish/pallas_call | solution.py:414
